TPU v7x, 32 devices: a whole 2x2x4 slice. The times are simulated.
32 devices in a mesh: section: 4 (over z), tm: 4 (over y, x), batch: 2 (over core).
Axes of the slice: x: 2, y: 2, z: 4, core: 2. Of those that a mesh axis runs over, the one named last changes fastest.
Arguments:
- acts: bfloat16 [4, 4, 8, 6, 10240], P('section', 'batch', 'tm'), may hold values from -6 to 6
- cot: bfloat16 [4, 8, 6, 10240], P('batch', 'tm'), may hold values from -6 to 6
- spatial_weight: bfloat16 [4, 9, 64, 64], P('section'), may hold values from -0.25 to 0.25
- temporal_weight: bfloat16 [4, 3, 64, 64], P('section'), may hold values from -0.4375 to 0.4375
Outputs:
- grad_in: bfloat16 [4, 4, 8, 6, 10240], P('section', 'batch', 'tm')
- grad_spatial: float32 [4, 9, 64, 64], P('section')
- grad_temporal: float32 [4, 3, 64, 64], P('section')
All inputs are finite; a program needn't handle non-finite values.
Results may differ from a plain program's by a relative error of at most 0.012.
Values may be sent and summed in bfloat16 or wider, within the bound.
A program may use at most 128 MiB of HBM per device.

v0:
```python
import functools

import jax
import jax.numpy as jnp
from jax import lax
from jax.experimental import pallas as pl
from jax.experimental.pallas import tpu as pltpu
from jax.sharding import PartitionSpec as P

DILATION = 2
ROWS = 8
LANES = 128
HALO = 3
MESH = pl.DeviceIdType.MESH


def neighbours(x):
    none = jnp.zeros_like(x[:, :1])
    after = jnp.concatenate([x[:, 1:], none], axis=1)
    before = jnp.concatenate([none, x[:, :-1]], axis=1)
    lane = lax.broadcasted_iota(jnp.int32, x.shape, 3)
    return jnp.where(lane < LANES // 2, after, before)


def flat(x):
    return x.reshape(-1, x.shape[-1])


def mm(a, b, dims):
    return lax.dot_general(a, b, (dims, ((), ())), preferred_element_type=jnp.float32)


def taps_of(d, dt, chans):
    def block(a, r, i, b):
        at = i * LANES + b * chans
        return a[r * chans : (r + 1) * chans, at : at + chans]

    taps = []
    for i in range(3):
        taps.append(block(d, 0, i, 1) + block(d, 3, i, 0))
        taps.append(block(d, 0, i, 0) + block(d, 1, i, 1))
        taps.append(block(d, 1, i, 0) + block(d, 2, i, 1))
    for k in range(3):
        taps.append(block(dt, 0, k, 0) + block(dt, 1, k, 1))
    return taps


def set_weights(ws_ref, wt_ref, fwd, back, time):
    chans = ws_ref.shape[-1]
    zero = jnp.zeros((chans, chans), jnp.bfloat16)
    for i in range(3):
        a, b, c = [ws_ref[3 * i + j] for j in range(3)]
        at = slice(i * LANES, (i + 1) * LANES)
        rows = [[b, a], [c, b], [zero, c], [a, zero]]
        fwd[:, at] = jnp.concatenate([jnp.concatenate(v, axis=1) for v in rows], axis=0)
        at = slice(i * 2 * LANES, (i + 1) * 2 * LANES)
        rows = [[b, a, zero, c], [c, b, a, zero]]
        back[:, at] = jnp.concatenate([jnp.concatenate(v, axis=1) for v in rows], axis=0)
        at = slice(i * LANES, (i + 1) * LANES)
        rows = [[wt_ref[i], zero], [zero, wt_ref[i]]]
        time[:, at] = jnp.concatenate([jnp.concatenate(v, axis=1) for v in rows], axis=0)


def pack(frame, stage, c, tiles, line, skip):
    tm, size = stage.shape[0], stage.shape[2]
    rows, width = frame.shape
    v = frame.astype(jnp.float32)
    for p in range(width // LANES):
        at = (p + HALO) * rows
        line[at : at + rows, :] = v[:, LANES * p : LANES * (p + 1)]
    for m in range(tm):
        at = (tiles * m + skip) * rows
        stage[m, c] = line[at : at + size, :].astype(jnp.bfloat16)


def spread(packed, loose, wide, rows, first, count):
    loose[...] = packed.astype(jnp.float32)
    for n in range(loose.shape[0]):
        for p in range(count):
            wide[n, first + p, 0:rows, :] = loose[n, rows * p : rows * (p + 1), :]


def kernel(
    sections, batches, tiles, acts, cot, ws_ref, wt_ref, out, spatial, temporal,
    x_stage, g_stage, x_buf, g_buf, r_buf, o_buf, home, fwd, back, time, acc, acc_t, ds,
    w_send, w_recv, w_piece, w_full,
    line, x_loose, g_loose, o_loose, x_wide, g_wide,
    x_sem, g_sem, z_sem, o_sem, w_sem, f_sem,
):
    tm = x_stage.shape[0]
    chains, frame_rows, width = acts.shape
    chans = ws_ref.shape[-1]
    pairs = x_wide.shape[1]
    tile_rows = o_buf.shape[2]
    group = tm * batches
    section, me, core = [lax.axis_index(a) for a in ("section", "tm", "batch")]
    rank = me * batches + core

    def member(e):
        other = lax.rem(rank + e, group)
        return other, (section, other // batches, lax.rem(other, batches))

    def peer(d):
        other = lax.rem(me + d, tm)
        return other, (section, other, core)

    barrier = pltpu.get_barrier_semaphore()
    for e in range(1, group):
        pl.semaphore_signal(barrier, inc=1, device_id=member(e)[1], device_id_type=MESH)

    @pl.when(section > 0)
    def _():
        pl.semaphore_signal(barrier, inc=1, device_id=(section - 1, me, core), device_id_type=MESH)

    @pl.when(section < sections - 1)
    def _():
        pl.semaphore_signal(barrier, inc=1, device_id=(section + 1, me, core), device_id_type=MESH)

    def copy(src, dst, sems, at, device):
        return pltpu.make_async_remote_copy(
            src_ref=src, dst_ref=dst, send_sem=sems.at[(0,) + at], recv_sem=sems.at[(1,) + at],
            device_id=device, device_id_type=MESH,
        )

    def x_copy(c, d):
        other, device = peer(d)
        return copy(x_stage.at[other, c], x_buf.at[c, me], x_sem, (c, d - 1), device)

    def g_copy(c, d):
        other, device = peer(d)
        return copy(g_stage.at[other, c], g_buf.at[c, me], g_sem, (c, d - 1), device)

    def z_copy(c):
        return copy(r_buf.at[c], g_buf.at[c], z_sem, (c,), (lax.max(section - 1, 0), me, core))

    def o_copy(c, d):
        other, device = peer(d)
        return copy(o_buf.at[c, other], home.at[c, me], o_sem, (c, d - 1), device)

    def w_copy(e):
        other, device = member(e)
        return copy(w_send.at[other], w_recv.at[rank], w_sem, (e - 1,), device)

    def f_copy(e):
        return copy(w_piece, w_full.at[rank], f_sem, (e - 1,), member(e)[1])

    line[...] = jnp.zeros_like(line)
    x_wide[...] = jnp.zeros_like(x_wide)
    g_wide[...] = jnp.zeros_like(g_wide)
    g_loose[...] = jnp.zeros_like(g_loose)
    pack(acts[0], x_stage, 0, tiles, line, 0)

    @pl.when(section == sections - 1)
    def _():
        pack(cot[0], g_stage, 0, tiles, line, 1)

    more = (section > 0).astype(jnp.int32) + (section < sections - 1).astype(jnp.int32)
    pl.semaphore_wait(barrier, group - 1 + more)

    def send(c, carry):
        @pl.when(c > 0)
        def _():
            pack(acts[c], x_stage, c, tiles, line, 0)

            @pl.when(section == sections - 1)
            def _():
                pack(cot[c], g_stage, c, tiles, line, 1)

        for d in range(1, tm):
            x_copy(c, d).start()
        x_buf[c, me] = x_stage[me, c]

        @pl.when(section == sections - 1)
        def _():
            for d in range(1, tm):
                g_copy(c, d).start()
            g_buf[c, me] = g_stage[me, c]

        return carry

    lax.fori_loop(0, chains, send, 0)
    set_weights(ws_ref, wt_ref, fwd, back, time)
    acc[...] = jnp.zeros_like(acc)
    acc_t[...] = jnp.zeros_like(acc_t)

    shape = (tm, pairs, ROWS, LANES)
    blank = jnp.zeros((1, pairs, ROWS, LANES), jnp.float32)
    centre = slice(HALO, HALO + tiles)

    def turn(c, carry):
        for d in range(1, tm):
            x_copy(c, d).wait_recv()
        spread(x_buf[c], x_loose, x_wide, frame_rows, 0, pairs)
        x = x_wide[...]
        xx = jnp.concatenate([x, neighbours(x)], axis=3)
        y = mm(flat(xx).astype(jnp.bfloat16), fwd[...], ((1,), (0,)))
        part = [y[:, LANES * i : LANES * (i + 1)].reshape(-1, ROWS, LANES) for i in range(3)]
        z = part[1] + pltpu.roll(part[0], 1, 1) + pltpu.roll(part[2], ROWS - 1, 1)
        z = z.reshape(shape)
        sig = jax.nn.sigmoid(z)
        h = z * sig
        slope = sig * (1.0 + z * (1.0 - sig))

        @pl.when(section == sections - 1)
        def _():
            for d in range(1, tm):
                g_copy(c, d).wait_recv()

        @pl.when(section < sections - 1)
        def _():
            z_copy(c).wait_recv()

        spread(g_buf[c], g_loose, g_wide, frame_rows, 1, pairs - 2)
        g = g_wide[...]
        g3 = jnp.concatenate(
            [
                jnp.concatenate([g[1:], blank], axis=0),
                g,
                jnp.concatenate([blank, g[:-1]], axis=0),
            ],
            axis=3,
        )
        gh = mm(flat(g3).astype(jnp.bfloat16), time[...], ((1,), (1,))).astype(jnp.bfloat16)
        gz = (gh.astype(jnp.float32).reshape(shape) * slope).astype(jnp.bfloat16)
        gz = gz.astype(jnp.float32)
        flat_gz = gz.reshape(-1, ROWS, LANES)
        gg = [
            pltpu.roll(flat_gz, ROWS - 1, 1).reshape(shape),
            gz,
            pltpu.roll(flat_gz, 1, 1).reshape(shape),
        ]
        sides = []
        for v in gg:
            sides += [v, neighbours(v)]
        sides = jnp.concatenate(sides, axis=3).astype(jnp.bfloat16)
        inner = mm(flat(sides), back[...], ((1,), (1,))).reshape(shape)
        place = me * tiles - HALO + lax.broadcasted_iota(jnp.int32, shape, 1)
        row = lax.broadcasted_iota(jnp.int32, shape, 2)
        inside = (place >= 0) & (place < width // LANES) & (row < frame_rows)
        result = jnp.where(inside, g + inner, 0.0)
        for n in range(tm):
            for p in range(pairs - 2):
                at = frame_rows * p
                g_loose[n, at : at + frame_rows, :] = result[n, p + 1, 0:frame_rows]
        r_buf[c] = g_loose[...].astype(jnp.bfloat16)

        @pl.when(section > 0)
        def _():
            z_copy(c).start()

        at = (HALO - 1) * frame_rows
        o_buf[c] = g_loose[:, at : at + tile_rows, :].astype(jnp.bfloat16)
        for d in range(1, tm):
            o_copy(c, d).start()
        home[c, me] = o_buf[c, me]
        hc = flat(h[:, centre]).astype(jnp.bfloat16)
        acc_t[...] += mm(hc, flat(g3[:, centre]).astype(jnp.bfloat16), ((0,), (0,)))
        gc = jnp.concatenate([v[:, centre] for v in gg], axis=3).astype(jnp.bfloat16)
        acc[...] += mm(flat(xx[:, centre]).astype(jnp.bfloat16), flat(gc), ((0,), (0,)))
        return carry

    lax.fori_loop(0, chains, turn, 0)

    taps = taps_of(acc[...], acc_t[...], chans)
    for k in range(6):
        ds[k * chans : (k + 1) * chans, :] = jnp.concatenate([taps[2 * k], taps[2 * k + 1]], axis=1)
    rows = w_send.shape[1]
    for k in range(group):
        w_send[k] = ds[k * rows : (k + 1) * rows, :].astype(jnp.bfloat16)
    for e in range(1, group):
        w_copy(e).start()
    w_recv[rank] = w_send[rank]

    def unpack(c, carry):
        for d in range(1, tm):
            o_copy(c, d).wait_recv()
        o_loose[...] = home[c].astype(jnp.float32)
        cut = [
            o_loose[m, frame_rows * p : frame_rows * (p + 1), :]
            for m in range(tm)
            for p in range(tiles)
        ]
        out[c] = jnp.concatenate(cut, axis=1).astype(jnp.bfloat16)
        return carry

    lax.fori_loop(0, chains - 1, unpack, 0)
    for e in range(1, group):
        w_copy(e).wait_recv()
    w_piece[...] = jnp.sum(w_recv[...].astype(jnp.float32), axis=0)
    for e in range(1, group):
        f_copy(e).start()
    w_full[rank] = w_piece[...]
    unpack(chains - 1, 0)

    for e in range(1, group):
        f_copy(e).wait_recv()
    for k in range(group):
        ds[k * rows : (k + 1) * rows, :] = w_full[k]
    for t in range(12):
        both = ds[(t // 2) * chans : (t // 2 + 1) * chans, :]
        half = both[:, (t % 2) * chans : (t % 2 + 1) * chans]
        if t < 9:
            spatial[t] = half
        else:
            temporal[t - 9] = half

    def finish(c, carry):
        for d in range(1, tm):
            x_copy(c, d).wait_send()
            o_copy(c, d).wait_send()

        @pl.when(section == sections - 1)
        def _():
            for d in range(1, tm):
                g_copy(c, d).wait_send()

        @pl.when(section > 0)
        def _():
            z_copy(c).wait_send()

        return carry

    lax.fori_loop(0, chains, finish, 0)
    for e in range(1, group):
        w_copy(e).wait_send()
        f_copy(e).wait_send()


def body(acts, cot, spatial_weight, temporal_weight):
    sections, tm, batches = [lax.axis_size(a) for a in ("section", "tm", "batch")]
    micro, local, rows, width = cot.shape
    chans = spatial_weight.shape[-1]
    chains = micro * local
    group = tm * batches
    tiles = width // LANES // tm
    pairs = tiles + 2 * HALO
    pairs += pairs % 2
    x_rows, g_rows, tile_rows = [-(-n * rows // 16) * 16 for n in (pairs, pairs - 2, tiles)]
    piece = 6 * chans // group
    bf16, f32 = jnp.bfloat16, jnp.float32
    vmem, dma = pltpu.VMEM, pltpu.SemaphoreType.DMA
    grad, spatial, temporal = pl.pallas_call(
        functools.partial(kernel, sections, batches, tiles),
        out_shape=[
            jax.ShapeDtypeStruct((chains, rows, width), bf16),
            jax.ShapeDtypeStruct((9, chans, chans), f32),
            jax.ShapeDtypeStruct((3, chans, chans), f32),
        ],
        in_specs=[pl.BlockSpec(memory_space=vmem)] * 4,
        out_specs=[pl.BlockSpec(memory_space=vmem)] * 3,
        scratch_shapes=[
            vmem((tm, chains, x_rows, LANES), bf16),
            vmem((tm, chains, g_rows, LANES), bf16),
            vmem((chains, tm, x_rows, LANES), bf16),
            vmem((chains, tm, g_rows, LANES), bf16),
            vmem((chains, tm, g_rows, LANES), bf16),
            vmem((chains, tm, tile_rows, LANES), bf16),
            vmem((chains, tm, tile_rows, LANES), bf16),
            vmem((2 * LANES, 3 * LANES), bf16),
            vmem((LANES, 6 * LANES), bf16),
            vmem((LANES, 3 * LANES), bf16),
            vmem((2 * LANES, 3 * LANES), f32),
            vmem((LANES, 3 * LANES), f32),
            vmem((6 * chans, LANES), f32),
            vmem((group, piece, LANES), bf16),
            vmem((group, piece, LANES), bf16),
            vmem((piece, LANES), f32),
            vmem((group, piece, LANES), f32),
            vmem(((width // LANES + HALO + pairs) * rows + 16, LANES), f32),
            vmem((tm, x_rows, LANES), f32),
            vmem((tm, g_rows, LANES), f32),
            vmem((tm, tile_rows, LANES), f32),
            vmem((tm, pairs, ROWS, LANES), f32),
            vmem((tm, pairs, ROWS, LANES), f32),
            dma((2, chains, tm - 1)),
            dma((2, chains, tm - 1)),
            dma((2, chains)),
            dma((2, chains, tm - 1)),
            dma((2, group - 1)),
            dma((2, group - 1)),
        ],
        compiler_params=pltpu.CompilerParams(
            collective_id=0, has_side_effects=True, vmem_limit_bytes=56 * 2**20
        ),
    )(acts.reshape(chains, rows, width), cot.reshape(chains, rows, width), spatial_weight[0], temporal_weight[0])
    return grad.reshape(acts.shape), spatial[None], temporal[None]


def solution(mesh):
    in_specs = (
        P("section", "batch", "tm", None, None),
        P("batch", "tm", None, None),
        P("section", None, None, None),
        P("section", None, None, None),
    )
    out_specs = (
        P("section", "batch", "tm", None, None),
        P("section", None, None, None),
        P("section", None, None, None),
    )
    return jax.shard_map(body, mesh=mesh, in_specs=in_specs, out_specs=out_specs, check_vma=False)
```

profile of v0, /device:TPU:0, one launch (start us, length us, event | category | flops | bytes accessed | tf_op | source)
XLA Modules:
  0.0 57.3 jit_solution(11210108538519389515)
XLA Ops:
  0.6 0.0 copy-start
  0.6 2.1 %copy.7 = bf16[1,2,2,6,10240]{4,3,2,1,0:T(8,128)(2,1)} copy(bf16[1,2,2,6,10240]{4,2,3,1,0:T(2,128)(2,1)} %param.4) | data formatting | bytes 983040 | tf_op args[0]
  2.7 0.0 copy-done
  2.7 1.0 %copy.8 = bf16[2,2,6,10240]{3,2,1,0:T(8,128)(2,1)} copy(bf16[2,2,6,10240]{3,1,2,0:T(2,128)(2,1)S(1)} %copy-done) | data formatting | bytes 983040 | tf_op args[1]
  3.7 49.5 %shard_map.67 = (bf16[4,6,10240]{2,1,0:T(8,128)(2,1)}, f32[9,64,64]{2,1,0:T(8,128)}, f32[3,64,64]{2,1,0:T(8,128)}) custom-call(bf16[4,6,10240]{2,1,0:T(8,128)(2,1)} %bitcast.7, bf16[4,6,10240]{2,1,0:T(8,128)(2,1)} %bitcast.8, bf16[9,64,64]{2,1,0:T(8,128)(2,1)} %bitcast.11, bf16[3,64,64]{2,1,0:T(8,128)(2,1)} %bitcast.13), custom_call_target="tpu_custom_call" | custom-call | tf_op jit(solution)/shard_map/pallas_call | solution.py:342
  53.2 0.0 copy-start.1
  53.2 2.4 %copy.9 = bf16[1,2,2,6,10240]{4,2,3,1,0:T(2,128)(2,1)} copy(bf16[1,2,2,6,10240]{4,3,2,1,0:T(8,128)(2,1)} %bitcast.9) | data formatting | bytes 983040
  55.7 0.0 copy-done.1
  55.7 0.0 copy-start.2
  55.7 0.7 %copy.12 = f32[1,9,64,64]{3,2,1,0:T(8,128)} copy(f32[1,9,64,64]{3,2,1,0:T(8,128)S(1)} %bitcast.10) | data formatting | bytes 294912
  56.4 0.2 copy-done.2
  56.6 0.6 %copy.13 = f32[1,3,64,64]{3,2,1,0:T(8,128)} copy(f32[1,3,64,64]{3,2,1,0:T(8,128)S(1)} %bitcast.12) | data formatting | bytes 98304
Async XLA Ops:
  0.6 2.1 %copy-start = (bf16[2,2,6,10240]{3,1,2,0:T(2,128)(2,1)S(1)}, bf16[2,2,6,10240]{3,1,2,0:T(2,128)(2,1)}, u32[]{:S(2)}) copy-start(bf16[2,2,6,10240]{3,1,2,0:T(2,128)(2,1)} %param.5) | copy-start | bytes 1474564
  53.2 2.4 %copy-start.1 = (f32[9,64,64]{2,1,0:T(8,128)S(1)}, f32[9,64,64]{2,1,0:T(8,128)}, u32[]{:S(2)}) copy-start(f32[9,64,64]{2,1,0:T(8,128)} %get-tuple-element.7) | copy-start | bytes 442372
  55.7 1.0 %copy-start.2 = (f32[3,64,64]{2,1,0:T(8,128)S(1)}, f32[3,64,64]{2,1,0:T(8,128)}, u32[]{:S(2)}) copy-start(f32[3,64,64]{2,1,0:T(8,128)} %get-tuple-element.8) | copy-start | bytes 147460
where the time goes:
time: 57.5 us; the launch traced here: 57.3 us
  Pallas kernels  49.5 us (86%)
  local copies, waits for them, and re-layouts  7.09 us (12%)
  between operations  0.66 us (1%)
    pallas_call x1, Pallas kernels, body(): pl.pallas_call(functools.partial(kernel, sections, batches, tiles), out_s...  49.5 us
    unnamed x11, local copies, waits for them, and re-layouts  7.09 us

commit v1 on v0

--- a/solution.py
+++ b/solution.py
@@ -61,13 +61,15 @@
         time[:, at] = jnp.concatenate([jnp.concatenate(v, axis=1) for v in rows], axis=0)
 
 
-def pack(frame, stage, c, tiles, line, skip):
+def pack(frames, stage, c, tiles, line, flatten, skip):
     tm, size = stage.shape[0], stage.shape[2]
-    rows, width = frame.shape
-    v = frame.astype(jnp.float32)
-    for p in range(width // LANES):
-        at = (p + HALO) * rows
-        line[at : at + rows, :] = v[:, LANES * p : LANES * (p + 1)]
+    rows, count = frames.shape[1], frames.shape[2]
+    local = stage.shape[1] // frames.shape[0]
+    pairs = count // local
+    flatten[...] = frames[c // local].astype(jnp.float32).reshape(flatten.shape)
+    for r in range(rows):
+        at = r * count + c % local
+        line[pl.ds(HALO * rows + r, pairs, stride=rows), :] = flatten[pl.ds(at, pairs, stride=local), :]
     for m in range(tm):
         at = (tiles * m + skip) * rows
         stage[m, c] = line[at : at + size, :].astype(jnp.bfloat16)
@@ -84,11 +86,14 @@
     sections, batches, tiles, acts, cot, ws_ref, wt_ref, out, spatial, temporal,
     x_stage, g_stage, x_buf, g_buf, r_buf, o_buf, home, fwd, back, time, acc, acc_t, ds,
     w_send, w_recv, w_piece, w_full,
-    line, x_loose, g_loose, o_loose, x_wide, g_wide,
+    line, flatten, x_loose, g_loose, o_loose, x_wide, g_wide,
     x_sem, g_sem, z_sem, o_sem, w_sem, f_sem,
 ):
     tm = x_stage.shape[0]
-    chains, frame_rows, width = acts.shape
+    micro, frame_rows, count, _ = acts.shape
+    chains = x_stage.shape[1]
+    local = chains // micro
+    width = count // local * LANES
     chans = ws_ref.shape[-1]
     pairs = x_wide.shape[1]
     tile_rows = o_buf.shape[2]
@@ -148,23 +153,22 @@
     x_wide[...] = jnp.zeros_like(x_wide)
     g_wide[...] = jnp.zeros_like(g_wide)
     g_loose[...] = jnp.zeros_like(g_loose)
-    pack(acts[0], x_stage, 0, tiles, line, 0)
+    pack(acts, x_stage, 0, tiles, line, flatten, 0)
 
     @pl.when(section == sections - 1)
     def _():
-        pack(cot[0], g_stage, 0, tiles, line, 1)
+        pack(cot, g_stage, 0, tiles, line, flatten, 1)
 
     more = (section > 0).astype(jnp.int32) + (section < sections - 1).astype(jnp.int32)
     pl.semaphore_wait(barrier, group - 1 + more)
 
-    def send(c, carry):
-        @pl.when(c > 0)
-        def _():
-            pack(acts[c], x_stage, c, tiles, line, 0)
+    def send(c):
+        if c > 0:
+            pack(acts, x_stage, c, tiles, line, flatten, 0)
 
             @pl.when(section == sections - 1)
             def _():
-                pack(cot[c], g_stage, c, tiles, line, 1)
+                pack(cot, g_stage, c, tiles, line, flatten, 1)
 
         for d in range(1, tm):
             x_copy(c, d).start()
@@ -176,9 +180,8 @@
                 g_copy(c, d).start()
             g_buf[c, me] = g_stage[me, c]
 
-        return carry
-
-    lax.fori_loop(0, chains, send, 0)
+    for c in range(chains):
+        send(c)
     set_weights(ws_ref, wt_ref, fwd, back, time)
     acc[...] = jnp.zeros_like(acc)
     acc_t[...] = jnp.zeros_like(acc_t)
@@ -271,26 +274,26 @@
         w_copy(e).start()
     w_recv[rank] = w_send[rank]
 
-    def unpack(c, carry):
+    def unpack(c):
         for d in range(1, tm):
             o_copy(c, d).wait_recv()
         o_loose[...] = home[c].astype(jnp.float32)
-        cut = [
-            o_loose[m, frame_rows * p : frame_rows * (p + 1), :]
-            for m in range(tm)
-            for p in range(tiles)
-        ]
-        out[c] = jnp.concatenate(cut, axis=1).astype(jnp.bfloat16)
-        return carry
-
-    lax.fori_loop(0, chains - 1, unpack, 0)
+        for m in range(tm):
+            for r in range(frame_rows):
+                at = r * count + m * tiles * local + c % local
+                flatten[pl.ds(at, tiles, stride=local), :] = o_loose[m, pl.ds(r, tiles, stride=frame_rows), :]
+        if c % local == local - 1:
+            out[c // local] = flatten[...].astype(jnp.bfloat16).reshape(frame_rows, count, LANES)
+
+    for c in range(chains - 1):
+        unpack(c)
     for e in range(1, group):
         w_copy(e).wait_recv()
     w_piece[...] = jnp.sum(w_recv[...].astype(jnp.float32), axis=0)
     for e in range(1, group):
         f_copy(e).start()
     w_full[rank] = w_piece[...]
-    unpack(chains - 1, 0)
+    unpack(chains - 1)
 
     for e in range(1, group):
         f_copy(e).wait_recv()
@@ -324,6 +327,18 @@
     for e in range(1, group):
         w_copy(e).wait_send()
         f_copy(e).wait_send()
+
+
+def tiled(a):
+    micro, local, rows, width = a.shape
+    a = a.reshape(micro, local, rows, width // LANES, LANES)
+    return a.transpose(0, 2, 3, 1, 4).reshape(micro, rows, width // LANES * local, LANES)
+
+
+def untiled(a, local):
+    micro, rows, count, _ = a.shape
+    a = a.reshape(micro, rows, count // local, local, LANES)
+    return a.transpose(0, 3, 1, 2, 4).reshape(micro, local, rows, count // local * LANES)
 
 
 def body(acts, cot, spatial_weight, temporal_weight):
@@ -342,7 +357,7 @@
     grad, spatial, temporal = pl.pallas_call(
         functools.partial(kernel, sections, batches, tiles),
         out_shape=[
-            jax.ShapeDtypeStruct((chains, rows, width), bf16),
+            jax.ShapeDtypeStruct((micro, rows, width // LANES * local, LANES), bf16),
             jax.ShapeDtypeStruct((9, chans, chans), f32),
             jax.ShapeDtypeStruct((3, chans, chans), f32),
         ],
@@ -367,6 +382,7 @@
             vmem((piece, LANES), f32),
             vmem((group, piece, LANES), f32),
             vmem(((width // LANES + HALO + pairs) * rows + 16, LANES), f32),
+            vmem((rows * width // LANES * local, LANES), f32),
             vmem((tm, x_rows, LANES), f32),
             vmem((tm, g_rows, LANES), f32),
             vmem((tm, tile_rows, LANES), f32),
@@ -382,8 +398,8 @@
         compiler_params=pltpu.CompilerParams(
             collective_id=0, has_side_effects=True, vmem_limit_bytes=56 * 2**20
         ),
-    )(acts.reshape(chains, rows, width), cot.reshape(chains, rows, width), spatial_weight[0], temporal_weight[0])
-    return grad.reshape(acts.shape), spatial[None], temporal[None]
+    )(tiled(acts[0]), tiled(cot), spatial_weight[0], temporal_weight[0])
+    return untiled(grad, local)[None], spatial[None], temporal[None]
 
 
 def solution(mesh):

time: 57.5 us -> 54 us (0.939)
  local copies, waits for them, and re-layouts: 7.09 us -> 3.8 us
    unnamed x11 -> x7, local copies, waits for them, and re-layouts: 7.09 us -> 3.8 us
where the time goes in v1:
time: 54 us; the launch traced here: 53.8 us
  Pallas kernels  49.3 us (91%)
  local copies, waits for them, and re-layouts  3.8 us (7%)
  between operations  0.65 us (1%)
    pallas_call x1, Pallas kernels, body(): pl.pallas_call(functools.partial(kernel, sections, batches, tiles), out_s...  49.3 us
    unnamed x7, local copies, waits for them, and re-layouts  3.8 us

profile of v1, /device:TPU:0, one launch (start us, length us, event | category | flops | bytes accessed | tf_op | source)
XLA Modules:
  0.0 53.8 jit_solution(669870543904530002)
XLA Ops:
  0.6 49.3 %shard_map.67 = (bf16[2,6,160,128]{3,2,1,0:T(8,128)(2,1)}, f32[9,64,64]{2,1,0:T(8,128)}, f32[3,64,64]{2,1,0:T(8,128)}) custom-call(bf16[2,6,160,128]{3,2,1,0:T(8,128)(2,1)} %bitcast.19, bf16[2,6,160,128]{3,2,1,0:T(8,128)(2,1)} %bitcast.20, bf16[9,64,64]{2,1,0:T(8,128)(2,1)} %bitcast.23, bf16[3,64,64]{2,1,0:T(8,128)(2,1)} %bitcast.25), custom_call_target="tpu_custom_call" | custom-call | tf_op jit(solution)/shard_map/pallas_call | solution.py:357
  50.0 0.0 copy-start
  50.0 2.2 %copy.13 = bf16[1,2,2,6,10240]{4,2,3,1,0:T(2,128)(2,1)} copy(bf16[1,2,2,6,10240]{4,2,3,1,0:T(2,128)(2,1)} %bitcast.21) | data formatting | bytes 983040
  52.2 0.0 copy-done
  52.2 0.0 copy-start.1
  52.2 0.7 %copy.14 = f32[1,9,64,64]{3,2,1,0:T(8,128)} copy(f32[1,9,64,64]{3,2,1,0:T(8,128)S(1)} %bitcast.22) | data formatting | bytes 294912
  52.9 0.2 copy-done.1
  53.1 0.6 %copy.15 = f32[1,3,64,64]{3,2,1,0:T(8,128)} copy(f32[1,3,64,64]{3,2,1,0:T(8,128)S(1)} %bitcast.24) | data formatting | bytes 98304
Async XLA Ops:
  50.0 2.2 %copy-start = (f32[9,64,64]{2,1,0:T(8,128)S(1)}, f32[9,64,64]{2,1,0:T(8,128)}, u32[]{:S(2)}) copy-start(f32[9,64,64]{2,1,0:T(8,128)} %get-tuple-element.7) | copy-start | bytes 442372
  52.2 1.0 %copy-start.1 = (f32[3,64,64]{2,1,0:T(8,128)S(1)}, f32[3,64,64]{2,1,0:T(8,128)}, u32[]{:S(2)}) copy-start(f32[3,64,64]{2,1,0:T(8,128)} %get-tuple-element.8) | copy-start | bytes 147460

commit v2 on v1

--- a/solution.py
+++ b/solution.py
@@ -82,7 +82,7 @@
             wide[n, first + p, 0:rows, :] = loose[n, rows * p : rows * (p + 1), :]
 
 
-def kernel(
+def tile_kernel(
     sections, batches, tiles, acts, cot, ws_ref, wt_ref, out, spatial, temporal,
     x_stage, g_stage, x_buf, g_buf, r_buf, o_buf, home, fwd, back, time, acc, acc_t, ds,
     w_send, w_recv, w_piece, w_full,
@@ -341,7 +341,7 @@
     return a.transpose(0, 3, 1, 2, 4).reshape(micro, local, rows, count // local * LANES)
 
 
-def body(acts, cot, spatial_weight, temporal_weight):
+def tile_plan(acts, cot, spatial_weight, temporal_weight):
     sections, tm, batches = [lax.axis_size(a) for a in ("section", "tm", "batch")]
     micro, local, rows, width = cot.shape
     chans = spatial_weight.shape[-1]
@@ -355,7 +355,7 @@
     bf16, f32 = jnp.bfloat16, jnp.float32
     vmem, dma = pltpu.VMEM, pltpu.SemaphoreType.DMA
     grad, spatial, temporal = pl.pallas_call(
-        functools.partial(kernel, sections, batches, tiles),
+        functools.partial(tile_kernel, sections, batches, tiles),
         out_shape=[
             jax.ShapeDtypeStruct((micro, rows, width // LANES * local, LANES), bf16),
             jax.ShapeDtypeStruct((9, chans, chans), f32),
@@ -399,6 +399,425 @@
             collective_id=0, has_side_effects=True, vmem_limit_bytes=56 * 2**20
         ),
     )(tiled(acts[0]), tiled(cot), spatial_weight[0], temporal_weight[0])
+    return grad, spatial, temporal
+
+STEP = 6
+TILE = 8
+
+
+def row_before(v):
+    sub = lax.broadcasted_iota(jnp.int32, v[:, :1].shape, 2)
+    first = jnp.where(sub >= ROWS // 2, pltpu.roll(v[:, -1:], ROWS // 2, 2), 0.0)
+    return jnp.concatenate([first, v[:, :-1]], axis=1)
+
+
+def row_after(v):
+    sub = lax.broadcasted_iota(jnp.int32, v[:, :1].shape, 2)
+    last = jnp.where(sub < ROWS // 2, pltpu.roll(v[:, :1], ROWS // 2, 2), 0.0)
+    return jnp.concatenate([v[:, 1:], last], axis=1)
+
+
+def beside(v):
+    count = v.shape[0] - 2
+    lane = lax.broadcasted_iota(jnp.int32, (count,) + v.shape[1:], 3)
+    return jnp.where(lane < LANES // 2, v[2:], v[:-2])
+
+
+def lanes(parts):
+    return jnp.concatenate([flat(v).astype(jnp.bfloat16) for v in parts], axis=1)
+
+
+def wide_weights(ws_ref, wt_ref, fwd, back, time):
+    chans = ws_ref.shape[-1]
+    zero = jnp.zeros((chans, chans), jnp.bfloat16)
+
+    def grid(rows):
+        return jnp.concatenate([jnp.concatenate(v, axis=1) for v in rows], axis=0)
+
+    for i in range(3):
+        a, b, c = [ws_ref[3 * i + j] for j in range(3)]
+        at = slice(i * LANES, (i + 1) * LANES)
+        fwd[:, at] = grid([[b, a], [c, b], [zero, c], [a, zero]])
+        back[at, :] = grid([[b, a, zero, c], [c, b, a, zero]])
+        time[:, at] = grid([[wt_ref[i], zero], [zero, wt_ref[i]]])
+
+
+def chain_kernel(
+    sections, batches, acts_hbm, cot_hbm, ws_hbm, wt_hbm, out, spatial, temporal,
+    acts, cot, ws, wt, x_stage, g_stage, x_in, g_in, xw, gw, res, g_buf, r_buf, o_stage, o_in,
+    loose, fwd, back, time, acc, acc_t, ds, w_send, w_recv, w_piece, w_full,
+    l_sem, x_sem, g_sem, z_sem, o_sem, w_sem, f_sem,
+):
+    micro, rows, count, _ = acts.shape
+    tiles, tm = x_in.shape[:2]
+    local = tm // micro
+    steps = g_buf.shape[0]
+    chans = ws.shape[-1]
+    pair = rows * tm
+    size = STEP * pair
+    group = tm * batches
+    section, me, core = [lax.axis_index(a) for a in ("section", "tm", "batch")]
+    last = section == sections - 1
+    lag = sections - 1 - section
+    rank = me * batches + core
+
+    def member(e):
+        other = lax.rem(rank + e, group)
+        return other, (section, other // batches, lax.rem(other, batches))
+
+    def peer(d):
+        other = lax.rem(me + d, tm)
+        return other, (section, other, core)
+
+    barrier = pltpu.get_barrier_semaphore()
+    for e in range(1, group):
+        pl.semaphore_signal(barrier, inc=1, device_id=member(e)[1], device_id_type=MESH)
+
+    @pl.when(section > 0)
+    def _():
+        pl.semaphore_signal(barrier, inc=1, device_id=(section - 1, me, core), device_id_type=MESH)
+
+    @pl.when(section < sections - 1)
+    def _():
+        pl.semaphore_signal(barrier, inc=1, device_id=(section + 1, me, core), device_id_type=MESH)
+
+    loads = [
+        pltpu.make_async_copy(a, b, l_sem.at[i])
+        for i, (a, b) in enumerate([(acts_hbm, acts), (cot_hbm, cot), (ws_hbm, ws), (wt_hbm, wt)])
+    ]
+    loads[0].start()
+
+    @pl.when(last)
+    def _():
+        loads[1].start()
+
+    loads[2].start()
+    loads[3].start()
+
+    def copy(src, dst, sems, at, device):
+        return pltpu.make_async_remote_copy(
+            src_ref=src, dst_ref=dst, send_sem=sems.at[(0,) + at], recv_sem=sems.at[(1,) + at],
+            device_id=device, device_id_type=MESH,
+        )
+
+    def x_copy(j, d):
+        other, device = peer(d)
+        return copy(x_stage.at[j, other], x_in.at[j, me], x_sem, (j, d - 1), device)
+
+    def g_copy(j, d):
+        other, device = peer(d)
+        return copy(g_stage.at[j, other], g_in.at[j, me], g_sem, (j, d - 1), device)
+
+    def z_copy(k):
+        return copy(r_buf.at[k], g_buf.at[k], z_sem, (k,), (lax.max(section - 1, 0), me, core))
+
+    def o_copy(j, d):
+        other, device = peer(d)
+        return copy(o_stage.at[j, other], o_in.at[j, me], o_sem, (j, d - 1), device)
+
+    def w_copy(e):
+        other, device = member(e)
+        return copy(w_send.at[other], w_recv.at[rank], w_sem, (e - 1,), device)
+
+    def f_copy(e):
+        return copy(w_piece, w_full.at[rank], f_sem, (e - 1,), member(e)[1])
+
+    def sub_of(r):
+        return r % (rows // 2) * ROWS + r // (rows // 2) * tm
+
+    span = TILE * local
+
+    def pack(frames, stage):
+        def tile(j, carry):
+            at = pl.ds(pl.multiple_of(span * j, span), span)
+            for n in range(micro):
+                for r in range(rows):
+                    loose[(n * rows + r) * span : (n * rows + r + 1) * span, :] = frames[n, r, at, :].astype(jnp.float32)
+            for n in range(micro):
+                for t in range(local):
+                    cut = [loose[pl.ds((n * rows + r) * span + t, TILE, stride=local), :] for r in range(rows)]
+                    stage[j, n * local + t] = jnp.concatenate(cut, axis=0).astype(jnp.bfloat16)
+            return carry
+
+        lax.fori_loop(0, tiles, tile, 0)
+
+    xw[...] = jnp.zeros_like(xw)
+    gw[...] = jnp.zeros_like(gw)
+    acc[...] = jnp.zeros_like(acc)
+    acc_t[...] = jnp.zeros_like(acc_t)
+
+    @pl.when(last)
+    def _():
+        loads[1].wait()
+        pack(cot, g_stage)
+
+    loads[0].wait()
+    pack(acts, x_stage)
+    more = (section > 0).astype(jnp.int32) + (section < sections - 1).astype(jnp.int32)
+    pl.semaphore_wait(barrier, group - 1 + more)
+
+    def send(j, carry):
+        for d in range(1, tm):
+            x_copy(j, d).start()
+        x_in[j, me] = x_stage[j, me]
+
+        @pl.when(last)
+        def _():
+            for d in range(1, tm):
+                g_copy(j, d).start()
+            g_in[j, me] = g_stage[j, me]
+
+        return carry
+
+    lax.fori_loop(0, tiles, send, 0)
+    loads[2].wait()
+    loads[3].wait()
+    wide_weights(ws, wt, fwd, back, time)
+
+    def spread(tile, wide, base):
+        for m in range(tm):
+            v = tile[m].astype(jnp.float32)
+            for r in range(rows):
+                at = base + (sub_of(r) + m)
+                wide[pl.ds(at, TILE, stride=pair), :] = v[TILE * r : TILE * (r + 1)]
+
+    def land(j, carry):
+        for d in range(1, tm):
+            x_copy(j, d).wait_recv()
+        spread(x_in[j], xw, (j * TILE + 1 + lag) * pair)
+
+        @pl.when(last)
+        def _():
+            for d in range(1, tm):
+                g_copy(j, d).wait_recv()
+            spread(g_in[j], gw, (j * TILE + 1) * pair)
+
+        return carry
+
+    def wanted(k):
+        return jnp.where(k < 0, 0, lax.min((STEP * (k + 1) + TILE) // TILE, tiles))
+
+    def ready(k):
+        return lax.max((STEP * (k + 1) + TILE - sections) // TILE - 1, 0)
+
+    shape = (STEP, rows // 2, ROWS, LANES)
+    sub = lax.broadcasted_iota(jnp.int32, shape, 2)
+    bin_at = sub % tm
+
+    def window(ref, first, many):
+        at = pl.multiple_of(first * pair, ROWS)
+        return ref[pl.ds(at, many * pair), :].reshape((many,) + shape[1:])
+
+    def give(j, carry):
+        base = (j * TILE + sections) * pair
+        for m in range(tm):
+            cut = [res[pl.ds(base + (sub_of(r) + m), TILE, stride=pair), :] for r in range(rows)]
+            o_stage[j, m] = jnp.concatenate(cut, axis=0).astype(jnp.bfloat16)
+        for d in range(1, tm):
+            o_copy(j, d).start()
+        o_in[j, me] = o_stage[j, me]
+        return carry
+
+    def turn(k, tail):
+        lax.fori_loop(wanted(k - 1), wanted(k), land, 0)
+        x = window(xw, STEP * k, STEP + 2)
+        xx = lanes([x[1:-1], beside(x)])
+        y = mm(xx, fwd[...], ((1,), (0,)))
+        part = [y[:, LANES * i : LANES * (i + 1)].reshape(shape) for i in range(3)]
+        z = part[1] + row_before(part[0]) + row_after(part[2])
+        sig = jax.nn.sigmoid(z)
+        h = z * sig
+        slope = sig * (1.0 + z * (1.0 - sig))
+
+        @pl.when(section < sections - 1)
+        def _():
+            z_copy(k).wait_recv()
+            at = pl.multiple_of((STEP * k + 1) * pair, ROWS)
+            gw[pl.ds(at, size), :] = g_buf[k].astype(jnp.float32)
+
+        held = window(gw, STEP * k, STEP + 1)
+        g = held[1:]
+        after = jnp.where(bin_at < tm - 1, pltpu.roll(g, ROWS - 1, 2), 0.0)
+        before = jnp.where(bin_at > 0, pltpu.roll(g, 1, 2), 0.0)
+        g3 = lanes([after, g, before])
+        gh = mm(g3, time[...], ((1,), (1,))).astype(jnp.bfloat16)
+        gz = (gh.astype(jnp.float32).reshape(shape) * slope).astype(jnp.bfloat16)
+        gz = gz.astype(jnp.float32)
+        sent = jnp.concatenate([tail, gz], axis=0)
+        y = mm(lanes([sent[1:-1], beside(sent)]), back[...], ((1,), (1,)))
+        part = [y[:, LANES * i : LANES * (i + 1)].reshape(shape) for i in range(3)]
+        inner = part[1] + row_after(part[0]) + row_before(part[2])
+        first = STEP * k - lag - 1
+        place = first + lax.broadcasted_iota(jnp.int32, shape, 0)
+        inside = (place >= 0) & (place < TILE * tiles)
+        result = flat(jnp.where(inside, held[:-1] + inner, 0.0))
+        r_buf[k] = result.astype(jnp.bfloat16)
+
+        @pl.when(section > 0)
+        def _():
+            z_copy(k).start()
+
+        res[pl.ds(pl.multiple_of((first + sections) * pair, ROWS), size), :] = result
+
+        lax.fori_loop(ready(k - 1), ready(k), give, 0)
+        acc_t[...] += mm(flat(h).astype(jnp.bfloat16), g3, ((0,), (0,)))
+        acc[...] += mm(xx, lanes([row_after(gz), gz, row_before(gz)]), ((0,), (0,)))
+        return gz[-2:]
+
+    lax.fori_loop(0, steps, turn, jnp.zeros((2,) + shape[1:], jnp.float32))
+
+    taps = taps_of(acc[...], acc_t[...], chans)
+    for k in range(6):
+        ds[k * chans : (k + 1) * chans, :] = jnp.concatenate([taps[2 * k], taps[2 * k + 1]], axis=1)
+    share = w_send.shape[1]
+    for k in range(group):
+        w_send[k] = ds[k * share : (k + 1) * share, :].astype(jnp.bfloat16)
+    for e in range(1, group):
+        w_copy(e).start()
+    w_recv[rank] = w_send[rank]
+
+    def unpack(j, carry):
+        for d in range(1, tm):
+            o_copy(j, d).wait_recv()
+        for c in range(tm):
+            v = o_in[j, c].astype(jnp.float32)
+            for r in range(rows):
+                at = (c // local * rows + r) * span + c % local
+                loose[pl.ds(at, TILE, stride=local), :] = v[TILE * r : TILE * (r + 1)]
+        at = pl.ds(pl.multiple_of(span * j, span), span)
+        for n in range(micro):
+            for r in range(rows):
+                v = loose[(n * rows + r) * span : (n * rows + r + 1) * span, :]
+                out[n, r, at, :] = v.astype(jnp.bfloat16)
+        return carry
+
+    lax.fori_loop(0, tiles - 2, unpack, 0)
+    for e in range(1, group):
+        w_copy(e).wait_recv()
+    w_piece[...] = jnp.sum(w_recv[...].astype(jnp.float32), axis=0)
+    for e in range(1, group):
+        f_copy(e).start()
+    w_full[rank] = w_piece[...]
+    lax.fori_loop(tiles - 2, tiles, unpack, 0)
+
+    for e in range(1, group):
+        f_copy(e).wait_recv()
+    for k in range(group):
+        ds[k * share : (k + 1) * share, :] = w_full[k]
+    for t in range(12):
+        both = ds[(t // 2) * chans : (t // 2 + 1) * chans, :]
+        half = both[:, (t % 2) * chans : (t % 2 + 1) * chans]
+        if t < 9:
+            spatial[t] = half
+        else:
+            temporal[t - 9] = half
+
+    def finish(j, carry):
+        for d in range(1, tm):
+            x_copy(j, d).wait_send()
+            o_copy(j, d).wait_send()
+
+        @pl.when(last)
+        def _():
+            for d in range(1, tm):
+                g_copy(j, d).wait_send()
+
+        return carry
+
+    lax.fori_loop(0, tiles, finish, 0)
+
+    @pl.when(section > 0)
+    def _():
+        def sent(k, carry):
+            z_copy(k).wait_send()
+            return carry
+
+        lax.fori_loop(0, steps, sent, 0)
+
+    for e in range(1, group):
+        w_copy(e).wait_send()
+        f_copy(e).wait_send()
+
+
+def chain_plan(acts, cot, spatial_weight, temporal_weight):
+    sections, tm, batches = [lax.axis_size(a) for a in ("section", "tm", "batch")]
+    micro, local, rows, width = cot.shape
+    chans = spatial_weight.shape[-1]
+    group = tm * batches
+    count = width // LANES
+    tiles = count // TILE
+    steps = -(-(count + sections) // STEP)
+    pair = rows * tm
+    piece = 6 * chans // group
+    bf16, f32 = jnp.bfloat16, jnp.float32
+    vmem, dma = pltpu.VMEM, pltpu.SemaphoreType.DMA
+    return pl.pallas_call(
+        functools.partial(chain_kernel, sections, batches),
+        out_shape=[
+            jax.ShapeDtypeStruct((micro, rows, count * local, LANES), bf16),
+            jax.ShapeDtypeStruct((9, chans, chans), f32),
+            jax.ShapeDtypeStruct((3, chans, chans), f32),
+        ],
+        in_specs=[pl.BlockSpec(memory_space=pl.ANY)] * 4,
+        out_specs=[pl.BlockSpec(memory_space=vmem)] * 3,
+        scratch_shapes=[
+            vmem((micro, rows, count * local, LANES), bf16),
+            vmem((micro, rows, count * local, LANES), bf16),
+            vmem((9, chans, chans), bf16),
+            vmem((3, chans, chans), bf16),
+        ]
+        + [vmem((tiles, tm, TILE * rows, LANES), bf16)] * 4
+        + [
+            vmem(((max(steps * STEP, count + sections) + 2) * pair, LANES), f32),
+            vmem(((steps * STEP + 1) * pair, LANES), f32),
+            vmem(((steps * STEP + sections) * pair, LANES), f32),
+            vmem((steps, STEP * pair, LANES), bf16),
+            vmem((steps, STEP * pair, LANES), bf16),
+            vmem((tiles, tm, TILE * rows, LANES), bf16),
+            vmem((tiles, tm, TILE * rows, LANES), bf16),
+            vmem((micro * rows * TILE * local, LANES), f32),
+            vmem((2 * LANES, 3 * LANES), bf16),
+            vmem((3 * LANES, 2 * LANES), bf16),
+            vmem((LANES, 3 * LANES), bf16),
+            vmem((2 * LANES, 3 * LANES), f32),
+            vmem((LANES, 3 * LANES), f32),
+            vmem((6 * chans, LANES), f32),
+            vmem((group, piece, LANES), bf16),
+            vmem((group, piece, LANES), bf16),
+            vmem((piece, LANES), f32),
+            vmem((group, piece, LANES), f32),
+            dma((4,)),
+            dma((2, tiles, tm - 1)),
+            dma((2, tiles, tm - 1)),
+            dma((2, steps)),
+            dma((2, tiles, tm - 1)),
+            dma((2, group - 1)),
+            dma((2, group - 1)),
+        ],
+        compiler_params=pltpu.CompilerParams(
+            collective_id=0, has_side_effects=True, vmem_limit_bytes=56 * 2**20
+        ),
+    )(tiled(acts[0]), tiled(cot), spatial_weight[0], temporal_weight[0])
+
+
+def hand_over(*refs):
+    half = len(refs) // 2
+    for a, b in zip(refs[:half], refs[half:]):
+        b[...] = a[...]
+
+
+def settle(arrays):
+    spec = [pl.BlockSpec(memory_space=pltpu.VMEM)] * len(arrays)
+    shapes = [jax.ShapeDtypeStruct(a.shape, a.dtype) for a in arrays]
+    return pl.pallas_call(hand_over, out_shape=shapes, in_specs=spec, out_specs=spec)(*arrays)
+
+
+def body(acts, cot, spatial_weight, temporal_weight):
+    tm, (micro, local, rows, width) = lax.axis_size("tm"), cot.shape
+    one_chain_each = tm == micro * local and 2 * tm == ROWS
+    whole = rows % 2 == 0 and width % (TILE * LANES) == 0 and TILE * local % 16 == 0 and TILE * rows % 16 == 0
+    plan = chain_plan if one_chain_each and whole and local == DILATION else tile_plan
+    grad, spatial, temporal = settle(plan(acts, cot, spatial_weight, temporal_weight))
     return untiled(grad, local)[None], spatial[None], temporal[None]
 
 

time: 54 us -> 47.3 us (0.88)
  local copies, waits for them, and re-layouts: 3.8 us -> 0 us
  Pallas kernels: 49.3 us -> 46.5 us
    unnamed x7 -> x0, local copies, waits for them, and re-layouts: 3.8 us -> none
    pallas_call x1 -> x2, Pallas kernels: 49.3 us -> 46.5 us  [the longest x1 44.4 us: chain_plan(): pl.pallas_call(functools.partial(chain_kernel, sections, batches), out_sh...]
where the time goes in v2:
time: 47.3 us; the launch traced here: 47.1 us
  Pallas kernels  46.5 us (98%)
  between operations  0.64 us (1%)
    pallas_call x1, Pallas kernels, chain_plan(): pl.pallas_call(functools.partial(chain_kernel, sections, batches), out_sh...  44.4 us
    pallas_call x1, Pallas kernels, settle(): pl.pallas_call(hand_over, out_shape=shapes, in_specs=spec, out_specs=spec)  2.05 us

profile of v2, /device:TPU:0, one launch (start us, length us, event | category | flops | bytes accessed | tf_op | source)
XLA Modules:
  0.0 47.1 jit_solution(15059652584887431089)
XLA Ops:
  0.6 44.4 %shard_map.67 = (bf16[2,6,160,128]{3,2,1,0:T(8,128)(2,1)}, f32[9,64,64]{2,1,0:T(8,128)}, f32[3,64,64]{2,1,0:T(8,128)}) custom-call(bf16[2,6,160,128]{3,2,1,0:T(8,128)(2,1)} %bitcast.19, bf16[2,6,160,128]{3,2,1,0:T(8,128)(2,1)} %bitcast.20, bf16[9,64,64]{2,1,0:T(8,128)(2,1)} %bitcast.21, bf16[3,64,64]{2,1,0:T(8,128)(2,1)} %bitcast.22), custom_call_target="tpu_custom_call" | custom-call | tf_op jit(solution)/shard_map/pallas_call | solution.py:754
  45.0 2.0 %shard_map.68 = (bf16[2,6,160,128]{3,2,1,0:T(8,128)(2,1)}, f32[9,64,64]{2,1,0:T(8,128)}, f32[3,64,64]{2,1,0:T(8,128)}) custom-call(bf16[2,6,160,128]{3,2,1,0:T(8,128)(2,1)} %get-tuple-element.9.refs_0_, f32[9,64,64]{2,1,0:T(8,128)} %get-tuple-element.10.refs_1_, f32[3,64,64]{2,1,0:T(8,128)} %get-tuple-element.11.refs_2_), custom_call_target="tpu_custom_call" | custom-call | tf_op jit(solution)/shard_map/pallas_call | solution.py:812

commit v3 on v2

--- a/solution.py
+++ b/solution.py
@@ -444,7 +444,7 @@
 
 def chain_kernel(
     sections, batches, acts_hbm, cot_hbm, ws_hbm, wt_hbm, out, spatial, temporal,
-    acts, cot, ws, wt, x_stage, g_stage, x_in, g_in, xw, gw, res, g_buf, r_buf, o_stage, o_in,
+    acts, cot, ws, wt, x_stage, g_stage, x_in, g_in, xw, gw, res, xs, hs, slopes, gs, ggs, g_buf, r_buf, o_stage, o_in,
     loose, fwd, back, time, acc, acc_t, ds, w_send, w_recv, w_piece, w_full,
     l_sem, x_sem, g_sem, z_sem, o_sem, w_sem, f_sem,
 ):
@@ -609,16 +609,17 @@
         return ref[pl.ds(at, many * pair), :].reshape((many,) + shape[1:])
 
     def give(j, carry):
-        base = (j * TILE + sections) * pair
+        third = rows // 2 * TILE
         for m in range(tm):
-            cut = [res[pl.ds(base + (sub_of(r) + m), TILE, stride=pair), :] for r in range(rows)]
+            at = [pl.multiple_of((j + 1) * TILE * pair + (a * tm + m) * third, TILE) for a in range(2)]
+            cut = [res[pl.ds(i, third), :] for i in at]
             o_stage[j, m] = jnp.concatenate(cut, axis=0).astype(jnp.bfloat16)
         for d in range(1, tm):
             o_copy(j, d).start()
         o_in[j, me] = o_stage[j, me]
         return carry
 
-    def turn(k, tail):
+    def ahead(k, carry):
         lax.fori_loop(wanted(k - 1), wanted(k), land, 0)
         x = window(xw, STEP * k, STEP + 2)
         xx = lanes([x[1:-1], beside(x)])
@@ -627,7 +628,20 @@
         z = part[1] + row_before(part[0]) + row_after(part[2])
         sig = jax.nn.sigmoid(z)
         h = z * sig
-        slope = sig * (1.0 + z * (1.0 - sig))
+        xs[k] = xx
+        hs[k] = flat(h).astype(jnp.bfloat16)
+        slopes[k] = flat(sig * (1.0 + z * (1.0 - sig)))
+        return carry
+
+    def grads(k, carry):
+        acc_t[...] += mm(hs[k], gs[k], ((0,), (0,)))
+        acc[...] += mm(xs[k], ggs[k], ((0,), (0,)))
+        return carry
+
+    def turn(k, tail):
+        @pl.when(last)
+        def _():
+            ahead(k, 0)
 
         @pl.when(section < sections - 1)
         def _():
@@ -641,7 +655,7 @@
         before = jnp.where(bin_at > 0, pltpu.roll(g, 1, 2), 0.0)
         g3 = lanes([after, g, before])
         gh = mm(g3, time[...], ((1,), (1,))).astype(jnp.bfloat16)
-        gz = (gh.astype(jnp.float32).reshape(shape) * slope).astype(jnp.bfloat16)
+        gz = (gh.astype(jnp.float32) * slopes[k]).reshape(shape).astype(jnp.bfloat16)
         gz = gz.astype(jnp.float32)
         sent = jnp.concatenate([tail, gz], axis=0)
         y = mm(lanes([sent[1:-1], beside(sent)]), back[...], ((1,), (1,)))
@@ -650,21 +664,38 @@
         first = STEP * k - lag - 1
         place = first + lax.broadcasted_iota(jnp.int32, shape, 0)
         inside = (place >= 0) & (place < TILE * tiles)
-        result = flat(jnp.where(inside, held[:-1] + inner, 0.0))
-        r_buf[k] = result.astype(jnp.bfloat16)
+        result = jnp.where(inside, held[:-1] + inner, 0.0)
+        r_buf[k] = flat(result).astype(jnp.bfloat16)
 
         @pl.when(section > 0)
         def _():
             z_copy(k).start()
 
-        res[pl.ds(pl.multiple_of((first + sections) * pair, ROWS), size), :] = result
+        for i in range(STEP):
+            q = first + TILE + i
+            at = q // TILE * (TILE * pair) + q % TILE
+            for b in range(rows // 2):
+                res[pl.ds(at + b * TILE, ROWS, stride=rows // 2 * TILE), :] = result[i, b]
 
         lax.fori_loop(ready(k - 1), ready(k), give, 0)
-        acc_t[...] += mm(flat(h).astype(jnp.bfloat16), g3, ((0,), (0,)))
-        acc[...] += mm(xx, lanes([row_after(gz), gz, row_before(gz)]), ((0,), (0,)))
+        gs[k] = g3
+        ggs[k] = lanes([row_after(gz), gz, row_before(gz)])
+
+        @pl.when(section < sections - 1)
+        def _():
+            grads(k, 0)
+
         return gz[-2:]
 
+    @pl.when(section < sections - 1)
+    def _():
+        lax.fori_loop(0, steps, ahead, 0)
+
     lax.fori_loop(0, steps, turn, jnp.zeros((2,) + shape[1:], jnp.float32))
+
+    @pl.when(last)
+    def _():
+        lax.fori_loop(0, steps, grads, 0)
 
     taps = taps_of(acc[...], acc_t[...], chans)
     for k in range(6):
@@ -694,16 +725,40 @@
     lax.fori_loop(0, tiles - 2, unpack, 0)
     for e in range(1, group):
         w_copy(e).wait_recv()
-    w_piece[...] = jnp.sum(w_recv[...].astype(jnp.float32), axis=0)
+    w_piece[...] = jnp.sum(w_recv[...].astype(jnp.float32), axis=0).astype(jnp.bfloat16)
     for e in range(1, group):
         f_copy(e).start()
     w_full[rank] = w_piece[...]
     lax.fori_loop(tiles - 2, tiles, unpack, 0)
 
+    def finish(j, carry):
+        for d in range(1, tm):
+            x_copy(j, d).wait_send()
+            o_copy(j, d).wait_send()
+
+        @pl.when(last)
+        def _():
+            for d in range(1, tm):
+                g_copy(j, d).wait_send()
+
+        return carry
+
+    lax.fori_loop(0, tiles, finish, 0)
+
+    @pl.when(section > 0)
+    def _():
+        def sent(k, carry):
+            z_copy(k).wait_send()
+            return carry
+
+        lax.fori_loop(0, steps, sent, 0)
+
+    for e in range(1, group):
+        w_copy(e).wait_send()
     for e in range(1, group):
         f_copy(e).wait_recv()
     for k in range(group):
-        ds[k * share : (k + 1) * share, :] = w_full[k]
+        ds[k * share : (k + 1) * share, :] = w_full[k].astype(jnp.float32)
     for t in range(12):
         both = ds[(t // 2) * chans : (t // 2 + 1) * chans, :]
         half = both[:, (t % 2) * chans : (t % 2 + 1) * chans]
@@ -711,31 +766,7 @@
             spatial[t] = half
         else:
             temporal[t - 9] = half
-
-    def finish(j, carry):
-        for d in range(1, tm):
-            x_copy(j, d).wait_send()
-            o_copy(j, d).wait_send()
-
-        @pl.when(last)
-        def _():
-            for d in range(1, tm):
-                g_copy(j, d).wait_send()
-
-        return carry
-
-    lax.fori_loop(0, tiles, finish, 0)
-
-    @pl.when(section > 0)
-    def _():
-        def sent(k, carry):
-            z_copy(k).wait_send()
-            return carry
-
-        lax.fori_loop(0, steps, sent, 0)
-
-    for e in range(1, group):
-        w_copy(e).wait_send()
+    for e in range(1, group):
         f_copy(e).wait_send()
 
 
@@ -754,9 +785,9 @@
     return pl.pallas_call(
         functools.partial(chain_kernel, sections, batches),
         out_shape=[
-            jax.ShapeDtypeStruct((micro, rows, count * local, LANES), bf16),
-            jax.ShapeDtypeStruct((9, chans, chans), f32),
-            jax.ShapeDtypeStruct((3, chans, chans), f32),
+            vmem((micro, rows, count * local, LANES), bf16),
+            vmem((9, chans, chans), f32),
+            vmem((3, chans, chans), f32),
         ],
         in_specs=[pl.BlockSpec(memory_space=pl.ANY)] * 4,
         out_specs=[pl.BlockSpec(memory_space=vmem)] * 3,
@@ -770,7 +801,12 @@
         + [
             vmem(((max(steps * STEP, count + sections) + 2) * pair, LANES), f32),
             vmem(((steps * STEP + 1) * pair, LANES), f32),
-            vmem(((steps * STEP + sections) * pair, LANES), f32),
+            vmem(((tiles + 2) * TILE * pair, LANES), f32),
+            vmem((steps, STEP * pair, 2 * LANES), bf16),
+            vmem((steps, STEP * pair, LANES), bf16),
+            vmem((steps, STEP * pair, LANES), f32),
+            vmem((steps, STEP * pair, 3 * LANES), bf16),
+            vmem((steps, STEP * pair, 3 * LANES), bf16),
             vmem((steps, STEP * pair, LANES), bf16),
             vmem((steps, STEP * pair, LANES), bf16),
             vmem((tiles, tm, TILE * rows, LANES), bf16),
@@ -784,8 +820,8 @@
             vmem((6 * chans, LANES), f32),
             vmem((group, piece, LANES), bf16),
             vmem((group, piece, LANES), bf16),
-            vmem((piece, LANES), f32),
-            vmem((group, piece, LANES), f32),
+            vmem((piece, LANES), bf16),
+            vmem((group, piece, LANES), bf16),
             dma((4,)),
             dma((2, tiles, tm - 1)),
             dma((2, tiles, tm - 1)),
@@ -801,15 +837,23 @@
 
 
 def hand_over(*refs):
-    half = len(refs) // 2
-    for a, b in zip(refs[:half], refs[half:]):
-        b[...] = a[...]
+    count = len(refs) // 2
+    copies = [pltpu.make_async_copy(refs[i], refs[count + i], refs[-1].at[i]) for i in range(count)]
+    for c in copies:
+        c.start()
+    for c in copies:
+        c.wait()
 
 
 def settle(arrays):
-    spec = [pl.BlockSpec(memory_space=pltpu.VMEM)] * len(arrays)
-    shapes = [jax.ShapeDtypeStruct(a.shape, a.dtype) for a in arrays]
-    return pl.pallas_call(hand_over, out_shape=shapes, in_specs=spec, out_specs=spec)(*arrays)
+    count = len(arrays)
+    return pl.pallas_call(
+        hand_over,
+        out_shape=[jax.ShapeDtypeStruct(a.shape, a.dtype) for a in arrays],
+        in_specs=[pl.BlockSpec(memory_space=pltpu.VMEM)] * count,
+        out_specs=[pl.BlockSpec(memory_space=pl.ANY)] * count,
+        scratch_shapes=[pltpu.SemaphoreType.DMA((count,))],
+    )(*[pltpu.with_memory_space_constraint(a, pltpu.VMEM) for a in arrays])
 
 
 def body(acts, cot, spatial_weight, temporal_weight):

time: 47.3 us -> 42.8 us (0.905)
  Pallas kernels: 46.5 us -> 42 us
    pallas_call x1, Pallas kernels: 44.4 us -> 41.1 us  [chain_plan(): pl.pallas_call(functools.partial(chain_kernel, sections, batches), out_sh...]
    pallas_call x1, Pallas kernels: 2.05 us -> 0.93 us  [settle(): pl.pallas_call(hand_over, out_shape=[jax.ShapeDtypeStruct(a.shape, a.dtyp...]
where the time goes in v3:
time: 42.8 us; the launch traced here: 42.6 us
  Pallas kernels  42 us (98%)
  between operations  0.64 us (1%)
    pallas_call x1, Pallas kernels, chain_plan(): pl.pallas_call(functools.partial(chain_kernel, sections, batches), out_sh...  41.1 us
    pallas_call x1, Pallas kernels, settle(): pl.pallas_call(hand_over, out_shape=[jax.ShapeDtypeStruct(a.shape, a.dtyp...  0.93 us

profile of v3, /device:TPU:0, one launch (start us, length us, event | category | flops | bytes accessed | tf_op | source)
XLA Modules:
  0.0 42.6 jit_solution(17397423148986867590)
XLA Ops:
  0.6 41.1 %shard_map.67 = (bf16[2,6,160,128]{3,2,1,0:T(8,128)(2,1)S(1)}, f32[9,64,64]{2,1,0:T(8,128)S(1)}, f32[3,64,64]{2,1,0:T(8,128)S(1)}) custom-call(bf16[2,6,160,128]{3,2,1,0:T(8,128)(2,1)} %bitcast.19, bf16[2,6,160,128]{3,2,1,0:T(8,128)(2,1)} %bitcast.20, bf16[9,64,64]{2,1,0:T(8,128)(2,1)} %bitcast.21, bf16[3,64,64]{2,1,0:T(8,128)(2,1)} %bitcast.22), custom_call_target="tpu_custom_call" | custom-call | tf_op jit(solution)/shard_map/pallas_call | solution.py:785
  41.7 0.9 %shard_map.68 = (bf16[2,6,160,128]{3,2,1,0:T(8,128)(2,1)}, f32[9,64,64]{2,1,0:T(8,128)}, f32[3,64,64]{2,1,0:T(8,128)}) custom-call(bf16[2,6,160,128]{3,2,1,0:T(8,128)(2,1)S(1)} %get-tuple-element.9.refs_0_, f32[9,64,64]{2,1,0:T(8,128)S(1)} %get-tuple-element.10.refs_1_, f32[3,64,64]{2,1,0:T(8,128)S(1)} %get-tuple-element.11.refs_2_), custom_call_target="tpu_custom_call" | custom-call | tf_op jit(solution)/shard_map/pallas_call | solution.py:850

commit v4 on v3

--- a/solution.py
+++ b/solution.py
@@ -403,6 +403,7 @@
 
 STEP = 6
 TILE = 8
+EARLY = 4
 
 
 def row_before(v):
@@ -440,6 +441,18 @@
         fwd[:, at] = grid([[b, a], [c, b], [zero, c], [a, zero]])
         back[at, :] = grid([[b, a, zero, c], [c, b, a, zero]])
         time[:, at] = grid([[wt_ref[i], zero], [zero, wt_ref[i]]])
+
+
+def folded(d, dt, chans):
+    low = lax.broadcasted_iota(jnp.int32, (chans, LANES), 1) < chans
+
+    def both(ref, i, a, b):
+        at = slice(i * LANES, (i + 1) * LANES)
+        v = jnp.where(low, ref[a * chans : (a + 1) * chans, at], ref[b * chans : (b + 1) * chans, at])
+        return v + pltpu.roll(v, chans, 1)
+
+    taps = [both(d, i, *rows) for i in range(3) for rows in ((3, 0), (0, 1), (1, 2))]
+    return taps + [both(dt, k, 0, 1) for k in range(3)]
 
 
 def chain_kernel(
@@ -458,6 +471,8 @@
     group = tm * batches
     section, me, core = [lax.axis_index(a) for a in ("section", "tm", "batch")]
     last = section == sections - 1
+    busy = section >= sections - 2
+    early = jnp.where(last, 1, jnp.where(busy, min(EARLY, steps), steps))
     lag = sections - 1 - section
     rank = me * batches + core
 
@@ -505,8 +520,8 @@
         return copy(x_stage.at[j, other], x_in.at[j, me], x_sem, (j, d - 1), device)
 
     def g_copy(j, d):
-        other, device = peer(d)
-        return copy(g_stage.at[j, other], g_in.at[j, me], g_sem, (j, d - 1), device)
+        other = peer(d)[0]
+        return copy(g_stage.at[j, other], g_in.at[j, me], g_sem, (j, d - 1), (section, other, core))
 
     def z_copy(k):
         return copy(r_buf.at[k], g_buf.at[k], z_sem, (k,), (lax.max(section - 1, 0), me, core))
@@ -527,49 +542,43 @@
 
     span = TILE * local
 
-    def pack(frames, stage):
-        def tile(j, carry):
-            at = pl.ds(pl.multiple_of(span * j, span), span)
-            for n in range(micro):
-                for r in range(rows):
-                    loose[(n * rows + r) * span : (n * rows + r + 1) * span, :] = frames[n, r, at, :].astype(jnp.float32)
-            for n in range(micro):
-                for t in range(local):
-                    cut = [loose[pl.ds((n * rows + r) * span + t, TILE, stride=local), :] for r in range(rows)]
-                    stage[j, n * local + t] = jnp.concatenate(cut, axis=0).astype(jnp.bfloat16)
-            return carry
-
-        lax.fori_loop(0, tiles, tile, 0)
-
+    def pack(frames, stage, j):
+        at = pl.ds(pl.multiple_of(span * j, span), span)
+        for n in range(micro):
+            for r in range(rows):
+                loose[(n * rows + r) * span : (n * rows + r + 1) * span, :] = frames[n, r, at, :].astype(jnp.float32)
+        for n in range(micro):
+            for t in range(local):
+                cut = [loose[pl.ds((n * rows + r) * span + t, TILE, stride=local), :] for r in range(rows)]
+                stage[j, n * local + t] = jnp.concatenate(cut, axis=0).astype(jnp.bfloat16)
+
+    def send(j, carry):
+        @pl.when(last)
+        def _():
+            pack(cot, g_stage, j)
+            for d in range(1, tm):
+                g_copy(j, d).start()
+            g_in[j, me] = g_stage[j, me]
+
+        pack(acts, x_stage, j)
+        for d in range(1, tm):
+            x_copy(j, d).start()
+        x_in[j, me] = x_stage[j, me]
+        return carry
+
+    more = (section > 0).astype(jnp.int32) + (section < sections - 1).astype(jnp.int32)
+    pl.semaphore_wait(barrier, group - 1 + more)
+
+    @pl.when(last)
+    def _():
+        loads[1].wait()
+
+    loads[0].wait()
+    lax.fori_loop(0, tiles, send, 0)
     xw[...] = jnp.zeros_like(xw)
     gw[...] = jnp.zeros_like(gw)
     acc[...] = jnp.zeros_like(acc)
     acc_t[...] = jnp.zeros_like(acc_t)
-
-    @pl.when(last)
-    def _():
-        loads[1].wait()
-        pack(cot, g_stage)
-
-    loads[0].wait()
-    pack(acts, x_stage)
-    more = (section > 0).astype(jnp.int32) + (section < sections - 1).astype(jnp.int32)
-    pl.semaphore_wait(barrier, group - 1 + more)
-
-    def send(j, carry):
-        for d in range(1, tm):
-            x_copy(j, d).start()
-        x_in[j, me] = x_stage[j, me]
-
-        @pl.when(last)
-        def _():
-            for d in range(1, tm):
-                g_copy(j, d).start()
-            g_in[j, me] = g_stage[j, me]
-
-        return carry
-
-    lax.fori_loop(0, tiles, send, 0)
     loads[2].wait()
     loads[3].wait()
     wide_weights(ws, wt, fwd, back, time)
@@ -633,16 +642,13 @@
         slopes[k] = flat(sig * (1.0 + z * (1.0 - sig)))
         return carry
 
-    def grads(k, carry):
-        acc_t[...] += mm(hs[k], gs[k], ((0,), (0,)))
-        acc[...] += mm(xs[k], ggs[k], ((0,), (0,)))
+    def grads(i, carry):
+        two = pl.ds(2 * i, 2)
+        acc_t[...] += mm(flat(hs[two]), flat(gs[two]), ((0,), (0,)))
+        acc[...] += mm(flat(xs[two]), flat(ggs[two]), ((0,), (0,)))
         return carry
 
     def turn(k, tail):
-        @pl.when(last)
-        def _():
-            ahead(k, 0)
-
         @pl.when(section < sections - 1)
         def _():
             z_copy(k).wait_recv()
@@ -681,25 +687,27 @@
         gs[k] = g3
         ggs[k] = lanes([row_after(gz), gz, row_before(gz)])
 
-        @pl.when(section < sections - 1)
-        def _():
-            grads(k, 0)
+        @pl.when(busy & (k + early < steps))
+        def _():
+            ahead(k + early, 0)
+
+        @pl.when(~busy & (k % 2 == 1))
+        def _():
+            grads(k // 2, 0)
 
         return gz[-2:]
 
-    @pl.when(section < sections - 1)
+    lax.fori_loop(0, early, ahead, 0)
+    lax.fori_loop(0, steps, turn, jnp.zeros((2,) + shape[1:], jnp.float32))
+
+    @pl.when(busy)
     def _():
-        lax.fori_loop(0, steps, ahead, 0)
-
-    lax.fori_loop(0, steps, turn, jnp.zeros((2,) + shape[1:], jnp.float32))
-
-    @pl.when(last)
-    def _():
-        lax.fori_loop(0, steps, grads, 0)
-
-    taps = taps_of(acc[...], acc_t[...], chans)
+        lax.fori_loop(0, steps // 2, grads, 0)
+
+    taps = folded(acc, acc_t, chans)
+    low = lax.broadcasted_iota(jnp.int32, taps[0].shape, 1) < chans
     for k in range(6):
-        ds[k * chans : (k + 1) * chans, :] = jnp.concatenate([taps[2 * k], taps[2 * k + 1]], axis=1)
+        ds[k * chans : (k + 1) * chans, :] = jnp.where(low, taps[2 * k], taps[2 * k + 1])
     share = w_send.shape[1]
     for k in range(group):
         w_send[k] = ds[k * share : (k + 1) * share, :].astype(jnp.bfloat16)
@@ -760,8 +768,7 @@
     for k in range(group):
         ds[k * share : (k + 1) * share, :] = w_full[k].astype(jnp.float32)
     for t in range(12):
-        both = ds[(t // 2) * chans : (t // 2 + 1) * chans, :]
-        half = both[:, (t % 2) * chans : (t % 2 + 1) * chans]
+        half = ds[(t // 2) * chans : (t // 2 + 1) * chans, (t % 2) * chans : (t % 2 + 1) * chans]
         if t < 9:
             spatial[t] = half
         else:
@@ -777,7 +784,7 @@
     group = tm * batches
     count = width // LANES
     tiles = count // TILE
-    steps = -(-(count + sections) // STEP)
+    steps = -(-(count + sections) // (2 * STEP)) * 2
     pair = rows * tm
     piece = 6 * chans // group
     bf16, f32 = jnp.bfloat16, jnp.float32
@@ -838,7 +845,9 @@
 
 def hand_over(*refs):
     count = len(refs) // 2
-    copies = [pltpu.make_async_copy(refs[i], refs[count + i], refs[-1].at[i]) for i in range(count)]
+    pieces = [(refs[0].at[n], refs[count].at[n]) for n in range(refs[0].shape[0])]
+    pieces += [(refs[i], refs[count + i]) for i in range(1, count)]
+    copies = [pltpu.make_async_copy(a, b, refs[-1].at[i]) for i, (a, b) in enumerate(pieces)]
     for c in copies:
         c.start()
     for c in copies:
@@ -852,7 +861,7 @@
         out_shape=[jax.ShapeDtypeStruct(a.shape, a.dtype) for a in arrays],
         in_specs=[pl.BlockSpec(memory_space=pltpu.VMEM)] * count,
         out_specs=[pl.BlockSpec(memory_space=pl.ANY)] * count,
-        scratch_shapes=[pltpu.SemaphoreType.DMA((count,))],
+        scratch_shapes=[pltpu.SemaphoreType.DMA((arrays[0].shape[0] + count - 1,))],
     )(*[pltpu.with_memory_space_constraint(a, pltpu.VMEM) for a in arrays])
 
 

time: 42.8 us -> 42.5 us (level)
  no operation moved by 1% of the time
where the time goes in v4:
time: 42.5 us; the launch traced here: 42.4 us
  Pallas kernels  41.7 us (98%)
  between operations  0.64 us (2%)
    pallas_call x1, Pallas kernels, chain_plan(): pl.pallas_call(functools.partial(chain_kernel, sections, batches), out_sh...  40.8 us
    pallas_call x1, Pallas kernels, settle(): pl.pallas_call(hand_over, out_shape=[jax.ShapeDtypeStruct(a.shape, a.dtyp...  0.94 us

profile of v4, /device:TPU:0, one launch (start us, length us, event | category | flops | bytes accessed | tf_op | source)
XLA Modules:
  0.0 42.4 jit_solution(3927807833463758282)
XLA Ops:
  0.6 40.8 %shard_map.67 = (bf16[2,6,160,128]{3,2,1,0:T(8,128)(2,1)S(1)}, f32[9,64,64]{2,1,0:T(8,128)S(1)}, f32[3,64,64]{2,1,0:T(8,128)S(1)}) custom-call(bf16[2,6,160,128]{3,2,1,0:T(8,128)(2,1)} %bitcast.19, bf16[2,6,160,128]{3,2,1,0:T(8,128)(2,1)} %bitcast.20, bf16[9,64,64]{2,1,0:T(8,128)(2,1)} %bitcast.21, bf16[3,64,64]{2,1,0:T(8,128)(2,1)} %bitcast.22), custom_call_target="tpu_custom_call" | custom-call | tf_op jit(solution)/shard_map/pallas_call | solution.py:792
  41.4 0.9 %shard_map.68 = (bf16[2,6,160,128]{3,2,1,0:T(8,128)(2,1)}, f32[9,64,64]{2,1,0:T(8,128)}, f32[3,64,64]{2,1,0:T(8,128)}) custom-call(bf16[2,6,160,128]{3,2,1,0:T(8,128)(2,1)S(1)} %get-tuple-element.9.refs_0_, f32[9,64,64]{2,1,0:T(8,128)S(1)} %get-tuple-element.10.refs_1_, f32[3,64,64]{2,1,0:T(8,128)S(1)} %get-tuple-element.11.refs_2_), custom_call_target="tpu_custom_call" | custom-call | tf_op jit(solution)/shard_map/pallas_call | solution.py:859

commit v5 on v4

--- a/solution.py
+++ b/solution.py
@@ -808,7 +808,7 @@
         + [
             vmem(((max(steps * STEP, count + sections) + 2) * pair, LANES), f32),
             vmem(((steps * STEP + 1) * pair, LANES), f32),
-            vmem(((tiles + 2) * TILE * pair, LANES), f32),
+            vmem(((tiles + 3) * TILE * pair, LANES), f32),
             vmem((steps, STEP * pair, 2 * LANES), bf16),
             vmem((steps, STEP * pair, LANES), bf16),
             vmem((steps, STEP * pair, LANES), f32),
@@ -818,7 +818,7 @@
             vmem((steps, STEP * pair, LANES), bf16),
             vmem((tiles, tm, TILE * rows, LANES), bf16),
             vmem((tiles, tm, TILE * rows, LANES), bf16),
-            vmem((micro * rows * TILE * local, LANES), f32),
+            vmem((micro * rows * TILE * local + ROWS, LANES), f32),
             vmem((2 * LANES, 3 * LANES), bf16),
             vmem((3 * LANES, 2 * LANES), bf16),
             vmem((LANES, 3 * LANES), bf16),

time: 42.5 us -> 42.5 us (level)
  no operation moved by 1% of the time
where the time goes in v5:
time: 42.5 us; the launch traced here: 42.4 us
  Pallas kernels  41.7 us (98%)
  between operations  0.64 us (2%)
    pallas_call x1, Pallas kernels, chain_plan(): pl.pallas_call(functools.partial(chain_kernel, sections, batches), out_sh...  40.8 us
    pallas_call x1, Pallas kernels, settle(): pl.pallas_call(hand_over, out_shape=[jax.ShapeDtypeStruct(a.shape, a.dtyp...  0.94 us

profile of v5, /device:TPU:0, one launch (start us, length us, event | category | flops | bytes accessed | tf_op | source)
XLA Modules:
  0.0 42.4 jit_solution(631904836651752462)
XLA Ops:
  0.6 40.8 %shard_map.67 = (bf16[2,6,160,128]{3,2,1,0:T(8,128)(2,1)S(1)}, f32[9,64,64]{2,1,0:T(8,128)S(1)}, f32[3,64,64]{2,1,0:T(8,128)S(1)}) custom-call(bf16[2,6,160,128]{3,2,1,0:T(8,128)(2,1)} %bitcast.19, bf16[2,6,160,128]{3,2,1,0:T(8,128)(2,1)} %bitcast.20, bf16[9,64,64]{2,1,0:T(8,128)(2,1)} %bitcast.21, bf16[3,64,64]{2,1,0:T(8,128)(2,1)} %bitcast.22), custom_call_target="tpu_custom_call" | custom-call | tf_op jit(solution)/shard_map/pallas_call | solution.py:792
  41.4 0.9 %shard_map.68 = (bf16[2,6,160,128]{3,2,1,0:T(8,128)(2,1)}, f32[9,64,64]{2,1,0:T(8,128)}, f32[3,64,64]{2,1,0:T(8,128)}) custom-call(bf16[2,6,160,128]{3,2,1,0:T(8,128)(2,1)S(1)} %get-tuple-element.9.refs_0_, f32[9,64,64]{2,1,0:T(8,128)S(1)} %get-tuple-element.10.refs_1_, f32[3,64,64]{2,1,0:T(8,128)S(1)} %get-tuple-element.11.refs_2_), custom_call_target="tpu_custom_call" | custom-call | tf_op jit(solution)/shard_map/pallas_call | solution.py:859

commit v6 on v5

--- a/solution.py
+++ b/solution.py
@@ -552,29 +552,40 @@
                 cut = [loose[pl.ds((n * rows + r) * span + t, TILE, stride=local), :] for r in range(rows)]
                 stage[j, n * local + t] = jnp.concatenate(cut, axis=0).astype(jnp.bfloat16)
 
+    def fill(j, carry):
+        @pl.when(last)
+        def _():
+            pack(cot, g_stage, j)
+
+        pack(acts, x_stage, j)
+        return carry
+
     def send(j, carry):
         @pl.when(last)
         def _():
-            pack(cot, g_stage, j)
             for d in range(1, tm):
                 g_copy(j, d).start()
             g_in[j, me] = g_stage[j, me]
 
-        pack(acts, x_stage, j)
         for d in range(1, tm):
             x_copy(j, d).start()
         x_in[j, me] = x_stage[j, me]
         return carry
 
-    more = (section > 0).astype(jnp.int32) + (section < sections - 1).astype(jnp.int32)
-    pl.semaphore_wait(barrier, group - 1 + more)
+    def fill_and_send(j, carry):
+        return send(j, fill(j, carry))
 
     @pl.when(last)
     def _():
         loads[1].wait()
 
     loads[0].wait()
-    lax.fori_loop(0, tiles, send, 0)
+    first = min(4, tiles)
+    lax.fori_loop(0, first, fill, 0)
+    more = (section > 0).astype(jnp.int32) + (section < sections - 1).astype(jnp.int32)
+    pl.semaphore_wait(barrier, group - 1 + more)
+    lax.fori_loop(0, first, send, 0)
+    lax.fori_loop(first, tiles, fill_and_send, 0)
     xw[...] = jnp.zeros_like(xw)
     gw[...] = jnp.zeros_like(gw)
     acc[...] = jnp.zeros_like(acc)

time: 42.5 us -> 42.6 us (level)
  no operation moved by 1% of the time
where the time goes in v6:
time: 42.6 us; the launch traced here: 42.4 us
  Pallas kernels  41.8 us (98%)
  between operations  0.64 us (2%)
    pallas_call x1, Pallas kernels, chain_plan(): pl.pallas_call(functools.partial(chain_kernel, sections, batches), out_sh...  40.8 us
    pallas_call x1, Pallas kernels, settle(): pl.pallas_call(hand_over, out_shape=[jax.ShapeDtypeStruct(a.shape, a.dtyp...  0.94 us

profile of v6, /device:TPU:0, one launch (start us, length us, event | category | flops | bytes accessed | tf_op | source)
XLA Modules:
  0.0 42.4 jit_solution(627959469726463453)
XLA Ops:
  0.6 40.8 %shard_map.67 = (bf16[2,6,160,128]{3,2,1,0:T(8,128)(2,1)S(1)}, f32[9,64,64]{2,1,0:T(8,128)S(1)}, f32[3,64,64]{2,1,0:T(8,128)S(1)}) custom-call(bf16[2,6,160,128]{3,2,1,0:T(8,128)(2,1)} %bitcast.19, bf16[2,6,160,128]{3,2,1,0:T(8,128)(2,1)} %bitcast.20, bf16[9,64,64]{2,1,0:T(8,128)(2,1)} %bitcast.21, bf16[3,64,64]{2,1,0:T(8,128)(2,1)} %bitcast.22), custom_call_target="tpu_custom_call" | custom-call | tf_op jit(solution)/shard_map/pallas_call | solution.py:803
  41.5 0.9 %shard_map.68 = (bf16[2,6,160,128]{3,2,1,0:T(8,128)(2,1)}, f32[9,64,64]{2,1,0:T(8,128)}, f32[3,64,64]{2,1,0:T(8,128)}) custom-call(bf16[2,6,160,128]{3,2,1,0:T(8,128)(2,1)S(1)} %get-tuple-element.9.refs_0_, f32[9,64,64]{2,1,0:T(8,128)S(1)} %get-tuple-element.10.refs_1_, f32[3,64,64]{2,1,0:T(8,128)S(1)} %get-tuple-element.11.refs_2_), custom_call_target="tpu_custom_call" | custom-call | tf_op jit(solution)/shard_map/pallas_call | solution.py:870

commit v7 on v5

--- a/solution.py
+++ b/solution.py
@@ -481,7 +481,7 @@
         return other, (section, other // batches, lax.rem(other, batches))
 
     def peer(d):
-        other = lax.rem(me + d, tm)
+        other = tm - 1 - me if d == 1 else lax.rem(me + tm // 2, tm) if d == 2 else me + 1 - 2 * lax.rem(me, 2)
         return other, (section, other, core)
 
     barrier = pltpu.get_barrier_semaphore()

time: 42.5 us -> 42.5 us (level)
  no operation moved by 1% of the time
where the time goes in v7:
time: 42.5 us; the launch traced here: 42.4 us
  Pallas kernels  41.7 us (98%)
  between operations  0.64 us (2%)
    pallas_call x1, Pallas kernels, chain_plan(): pl.pallas_call(functools.partial(chain_kernel, sections, batches), out_sh...  40.8 us
    pallas_call x1, Pallas kernels, settle(): pl.pallas_call(hand_over, out_shape=[jax.ShapeDtypeStruct(a.shape, a.dtyp...  0.94 us

profile of v7, /device:TPU:0, one launch (start us, length us, event | category | flops | bytes accessed | tf_op | source)
XLA Modules:
  0.0 42.4 jit_solution(13658227139649504690)
XLA Ops:
  0.6 40.8 %shard_map.67 = (bf16[2,6,160,128]{3,2,1,0:T(8,128)(2,1)S(1)}, f32[9,64,64]{2,1,0:T(8,128)S(1)}, f32[3,64,64]{2,1,0:T(8,128)S(1)}) custom-call(bf16[2,6,160,128]{3,2,1,0:T(8,128)(2,1)} %bitcast.19, bf16[2,6,160,128]{3,2,1,0:T(8,128)(2,1)} %bitcast.20, bf16[9,64,64]{2,1,0:T(8,128)(2,1)} %bitcast.21, bf16[3,64,64]{2,1,0:T(8,128)(2,1)} %bitcast.22), custom_call_target="tpu_custom_call" | custom-call | tf_op jit(solution)/shard_map/pallas_call | solution.py:792
  41.4 0.9 %shard_map.68 = (bf16[2,6,160,128]{3,2,1,0:T(8,128)(2,1)}, f32[9,64,64]{2,1,0:T(8,128)}, f32[3,64,64]{2,1,0:T(8,128)}) custom-call(bf16[2,6,160,128]{3,2,1,0:T(8,128)(2,1)S(1)} %get-tuple-element.9.refs_0_, f32[9,64,64]{2,1,0:T(8,128)S(1)} %get-tuple-element.10.refs_1_, f32[3,64,64]{2,1,0:T(8,128)S(1)} %get-tuple-element.11.refs_2_), custom_call_target="tpu_custom_call" | custom-call | tf_op jit(solution)/shard_map/pallas_call | solution.py:859
